TPU v7x, 128 devices: a whole 4x4x4 slice. The times are simulated.
128 devices in a mesh: dp: 32 (over y, z, core), mp: 4 (over x).
Axes of the slice: x: 4, y: 4, z: 4, core: 2. Of those that a mesh axis runs over, the one named last changes fastest.
Arguments:
- hidden: bfloat16 [8192, 8192], P('dp', 'mp'), may hold values from -6 to 6
- base_query_rows: bfloat16 [8192, 8192], P('dp', 'mp'), may hold values from -6 to 6
- key_value_base: bfloat16 [8192, 2, 1024], P('dp', None, 'mp'), may hold values from -6 to 6
- key_value_pool: bfloat16 [8192, 2, 16, 1024], P('dp', None, None, 'mp'), may hold values from -28 to 28
- request_page_table: int32 [8192, 16], P('dp'), may hold values from 0 to 319
- context_length: int32 [8192], P('dp'), may hold values from 1 to 256
- handover_pages: int32 [1024, 2], P('dp'), may hold values from 0 to 255
- request_adapter: int32 [8192], P('dp'), may hold values from 0 to 511, as said below
- adapter_position: int32 [512], replicated, may hold values from 0 to 511, as said below
- adapter_down_weight: bfloat16 [512, 3, 64, 8192], P('dp', None, None, 'mp'), may hold values from -0.0625 to 0.0625
- query_up_weight: bfloat16 [512, 64, 8192], P('dp', None, 'mp'), may hold values from -0.75 to 0.75
- key_value_up: bfloat16 [512, 2, 64, 1024], P('dp', None, None, 'mp'), may hold values from -0.75 to 0.75
Outputs:
- attended: bfloat16 [8192, 8192], P('dp', 'mp')
Inputs may be any that keep to these rules, and one draw needn't show every extreme that they name: `request_adapter`: among the requests of one index of dp, at most 16 use adapters whose slots lie with one owner, and in every such block some owner has exactly 16 of them. `adapter_position`: each adapter has a slot of its own.
All inputs are finite; a program needn't handle non-finite values.
Results may differ from a plain program's by a relative error of at most 0.009.
Values may be sent and summed in bfloat16 or wider, within the bound.
A program may use at most 128 MiB of HBM per device.

v0:
```python
import math

import jax
import jax.numpy as jnp
from jax import lax
from jax.sharding import PartitionSpec as P

HEAD_SIZE = 128
PAGE_TOKENS = 16
MCAP = 2


adapter_scale = 0.5


def lookup(ids, table):
    hits = ids[:, None] == jnp.arange(table.shape[0], dtype=jnp.int32)[None, :]
    return jnp.sum(jnp.where(hits, table[None, :], 0), axis=1)


def route_rows(slot_rows, owners, owner_grouping, capacity):
    owner = slot_rows // owner_grouping
    marks = (owner[:, None] == jnp.arange(owners, dtype=jnp.int32)[None, :]).astype(jnp.int32)
    before = jnp.cumsum(marks, axis=0) - marks
    position = jnp.sum(before * marks, axis=1)
    return owner * capacity + position


def build_update_delta(
    flattened_rows,
    local_indices,
    adapter_down_weight,
    query_up_weight,
    key_value_up,
    reduce_rank_partial,
):
    slots_in = flattened_rows.shape[0]
    owner_grouping = adapter_down_weight.shape[0]
    adapter_rank_size = adapter_down_weight.shape[2]
    width_portion = flattened_rows.shape[1]
    query_part = query_up_weight.shape[2]
    kv_part = key_value_up.shape[3]
    flattened_down = adapter_down_weight.reshape(
        owner_grouping * 3 * adapter_rank_size, width_portion
    )
    projected = lax.dot_general(
        flattened_rows, flattened_down, (((1,), (1,)), ((), ())), preferred_element_type=jnp.float32
    )
    projected = projected.reshape(slots_in, owner_grouping, 3 * adapter_rank_size)
    picked = (
        local_indices[:, None] == jnp.arange(owner_grouping, dtype=jnp.int32)[None, :]
    ).astype(jnp.float32)
    partial_low = jnp.einsum("mk,mkc->mc", picked, projected)
    low = reduce_rank_partial(partial_low).astype(jnp.bfloat16)
    spread = (picked.astype(jnp.bfloat16)[:, :, None] * low[:, None, :]).reshape(
        slots_in, owner_grouping, 3, adapter_rank_size
    )
    query_delta_rows = jnp.dot(
        spread[:, :, 0, :].reshape(slots_in, owner_grouping * adapter_rank_size),
        query_up_weight.reshape(owner_grouping * adapter_rank_size, query_part),
        preferred_element_type=jnp.float32,
    )
    key_delta_rows = jnp.dot(
        spread[:, :, 1, :].reshape(slots_in, owner_grouping * adapter_rank_size),
        key_value_up[:, 0].reshape(owner_grouping * adapter_rank_size, kv_part),
        preferred_element_type=jnp.float32,
    )
    value_delta_rows = jnp.dot(
        spread[:, :, 2, :].reshape(slots_in, owner_grouping * adapter_rank_size),
        key_value_up[:, 1].reshape(owner_grouping * adapter_rank_size, kv_part),
        preferred_element_type=jnp.float32,
    )
    return (
        adapter_scale
        * jnp.concatenate([query_delta_rows, key_delta_rows, value_delta_rows], axis=1)
    ).astype(jnp.bfloat16)


def attend(query, key_new, value_new, key_pages, value_pages, lengths):
    count = query.shape[0]
    heads_kv = key_new.shape[1] // HEAD_SIZE
    groups = query.shape[1] // (heads_kv * HEAD_SIZE)
    keys = key_pages.reshape(count, -1, heads_kv, HEAD_SIZE)
    values = value_pages.reshape(count, -1, heads_kv, HEAD_SIZE)
    heads = query.reshape(count, heads_kv, groups, HEAD_SIZE)
    factor = HEAD_SIZE ** (-0.5)
    scores = jnp.einsum("bhgd,bthd->bhgt", heads, keys, preferred_element_type=jnp.float32) * factor
    own = (
        jnp.einsum(
            "bhgd,bhd->bhg",
            heads,
            key_new.reshape(count, heads_kv, HEAD_SIZE),
            preferred_element_type=jnp.float32,
        )
        * factor
    )
    valid = jnp.arange(keys.shape[1], dtype=jnp.int32)[None, :] < lengths[:, None]
    scores = jnp.where(valid[:, None, None, :], scores, -jnp.inf)
    top = jnp.maximum(jnp.max(scores, axis=-1), own)
    probs = jnp.exp(scores - top[..., None])
    own_p = jnp.exp(own - top)
    total = jnp.sum(probs, axis=-1) + own_p
    weights = (probs / total[..., None]).astype(jnp.bfloat16)
    own_w = (own_p / total).astype(jnp.bfloat16)
    out = jnp.einsum("bhgt,bthd->bhgd", weights, values, preferred_element_type=jnp.float32)
    out = out + own_w.astype(jnp.float32)[..., None] * value_new.reshape(
        count, heads_kv, 1, HEAD_SIZE
    ).astype(jnp.float32)
    return out.reshape(count, -1).astype(jnp.bfloat16)


def shards(
    hidden,
    base_query_rows,
    key_value_base,
    key_value_pool,
    request_page_table,
    context_length,
    handover_pages,
    request_adapter,
    adapter_position,
    adapter_down_weight,
    query_up_weight,
    key_value_up,
):
    owners = lax.axis_size("dp")
    me = lax.axis_index("dp")
    rows = hidden.shape[0]
    capacity = 2 * rows // owners
    owner_grouping = adapter_down_weight.shape[0]
    width_portion = hidden.shape[1]
    query_part = base_query_rows.shape[1]
    kv_part = key_value_base.shape[2]
    total_slots = owners * capacity
    slot_rows = lookup(request_adapter, adapter_position)
    target = route_rows(slot_rows, owners, owner_grouping, capacity)
    placed = target[None, :] == jnp.arange(total_slots, dtype=jnp.int32)[:, None]
    placement = placed.astype(jnp.bfloat16)
    send_rows = jnp.dot(placement, hidden, preferred_element_type=jnp.float32).astype(jnp.bfloat16)
    send_rows = send_rows.reshape(owners, capacity, width_portion)
    leaving_pages = key_value_pool[handover_pages]
    all_ids = lax.all_gather(request_adapter, "dp", axis=0, tiled=True)
    all_slots = lookup(all_ids, adapter_position).reshape(owners, rows)
    all_targets = jax.vmap(lambda s: route_rows(s, owners, owner_grouping, capacity))(all_slots)
    sources = jnp.arange(owners, dtype=jnp.int32)[:, None] * capacity
    where_to = jnp.where(
        all_slots // owner_grouping == me, all_targets % capacity + sources, total_slots
    )
    arriving_local = (
        jnp.zeros((total_slots,), jnp.int32)
        .at[where_to.reshape(-1)]
        .set((all_slots % owner_grouping).reshape(-1), mode="drop")
    )
    arrived = lax.all_to_all(send_rows, "dp", split_axis=0, concat_axis=0, tiled=True)
    migrated = lax.all_to_all(leaving_pages, "dp", split_axis=0, concat_axis=0, tiled=True)
    update_delta = build_update_delta(
        arrived.reshape(total_slots, width_portion),
        arriving_local,
        adapter_down_weight,
        query_up_weight,
        key_value_up,
        lambda partial_low: lax.psum(partial_low, "mp"),
    )
    returned = lax.all_to_all(
        update_delta.reshape(owners, capacity, query_part + 2 * kv_part),
        "dp",
        split_axis=0,
        concat_axis=0,
        tiled=True,
    )
    returned_flat = returned.reshape(total_slots, query_part + 2 * kv_part)
    own_delta = lax.dot_general(
        placement, returned_flat, (((0,), (0,)), ((), ())), preferred_element_type=jnp.float32
    )
    query = (base_query_rows.astype(jnp.float32) + own_delta[:, :query_part]).astype(jnp.bfloat16)
    fresh = (
        key_value_base.astype(jnp.float32) + own_delta[:, query_part:].reshape(rows, 2, kv_part)
    ).astype(jnp.bfloat16)
    arrived_pages = migrated.reshape(owners * MCAP, 2, PAGE_TOKENS, kv_part)
    key_store = jnp.concatenate([key_value_pool[:, 0], arrived_pages[:, 0]], axis=0)
    value_store = jnp.concatenate([key_value_pool[:, 1], arrived_pages[:, 1]], axis=0)
    block = math.gcd(rows, 64)
    count = rows // block

    def one_block(call_arguments):
        q_blk, f_blk, t_blk, l_blk = call_arguments
        return attend(q_blk, f_blk[:, 0], f_blk[:, 1], key_store[t_blk], value_store[t_blk], l_blk)

    out = lax.map(
        one_block,
        (
            query.reshape(count, block, query_part),
            fresh.reshape(count, block, 2, kv_part),
            request_page_table.reshape(count, block, -1),
            context_length.reshape(count, block),
        ),
    )
    return out.reshape(rows, query_part)


def solution(mesh):
    return jax.shard_map(
        shards,
        mesh=mesh,
        in_specs=(
            P("dp", "mp"),
            P("dp", "mp"),
            P("dp", None, "mp"),
            P("dp", None, None, "mp"),
            P("dp", None),
            P("dp"),
            P("dp", None),
            P("dp"),
            P(),
            P("dp", None, None, "mp"),
            P("dp", None, "mp"),
            P("dp", None, None, "mp"),
        ),
        out_specs=P("dp", "mp"),
        check_vma=False,
    )
```

profile of v0, /device:TPU:1, one launch (start us, length us, event | category | flops | bytes accessed | tf_op | source)
XLA Modules:
  0.0 461.7 jit_solution(7281419739457481494)
XLA Ops:
  4.0 9.7 %all-to-all-start = ((bf16[32,16,2048]{2,1,0:T(8,128)(2,1)}), bf16[32,16,2048]{2,1,0:T(8,128)(2,1)}, u32[]{:S(2)}, u32[]{:S(2)}) async-start(bf16[32,16,2048]{2,1,0:T(8,128)(2,1)} %bitcast.13), calls=%async_computation | async-start | bytes 4194304 | tf_op jit(solution)/shard_map/all_to_all | solution.py:154
  13.7 43.5 %all-gather = s32[32,1,256]{2,1,0:T(1,128)S(1)} all-gather(s32[1,1,256]{2,1,0:T(1,128)S(1)} %bitcast.203), channel_id=1, replica_groups=mesh['dp'=32,'mp'=4] {'dp'}, dimensions={0}, use_global_device_ids=true | all-gather | bytes 33792 | tf_op jit(solution)/shard_map/all_gather | solution.py:142
  60.9 18.4 %reduce-window.16 = s32[32,32,2,128]{3,1,2,0:T(8,128)S(1)} reduce-window(s32[32,32,2,128]{3,1,2,0:T(8,128)S(1)} %fusion.38, s32[]{:T(128)} %copy.223), window={size=1x1x1x128 pad=0_0x0_0x0_0x127_0}, to_apply=%region_5.6 | reduce-window | flops 33292288 | bytes 2097156 | tf_op jit(solution)/shard_map/reduce-window.2
  81.2 30.4 %scatter_custom_fusion = s32[512]{0:T(512)S(1)} fusion(s32[8192]{0:T(1024)S(1)} %bitcast.202, s32[8192]{0:T(1024)S(1)} %add_select_fusion, s32[]{:T(128)} %copy.223), kind=kCustom, calls=%fused_computation.125 | custom fusion | bytes 2052 | tf_op jit(solution)/shard_map/scatter | solution.py:152
  120.3 10.4 %multiply_reduce_fusion = f32[512,192]{0,1:T(8,128)S(1)} fusion(f32[512,16]{0,1:T(8,128)S(1)} %copy.161, bf16[512,2048,1]{1,0,2:T(8,128)(2,1)} %bitcast.15, bf16[16,192,2048]{2,1,0:T(8,128)(2,1)} %bitcast.204), kind=kOutput, calls=%fused_computation.34 | convolution fusion | flops 6445498368 | bytes 15106048 | tf_op jit(solution)/shard_map/dot_general | solution.py:46
  130.7 17.1 %all-reduce.1 = bf16[512,192]{0,1:T(8,128)(2,1)S(1)} all-reduce(f32[512,192]{0,1:T(8,128)S(1)} %multiply_reduce_fusion), channel_id=1, replica_groups=mesh['dp'=32,'mp'=4] {'mp'}, use_global_device_ids=true, to_apply=%region_9.10 | all-reduce | flops 98304 | bytes 589824 | tf_op jit(solution)/shard_map/psum | solution.py:162
  157.5 4.9 %fusion.65 = f32[32,16,2048]{2,1,0:T(8,128)S(1)} fusion(bf16[32,16,1024]{2,1,0:T(8,128)(2,1)} %dot_general.42, bf16[1024,2048,1]{1,0,2:T(8,128)(2,1)} %bitcast.205), kind=kOutput, calls=%fused_computation.132 | convolution fusion | flops 2147483648 | bytes 9437184 | tf_op jit(solution)/shard_map/dot_general | solution.py:58
  164.5 12.3 %all-to-all-start.1 = ((bf16[32,16,2560]{2,1,0:T(8,128)(2,1)}), bf16[32,16,2560]{2,1,0:T(8,128)(2,1)}, u32[]{:S(2)}, u32[]{:S(2)}) async-start(bf16[32,16,2560]{2,1,0:T(8,128)(2,1)} %fusion.23), calls=%async_computation.1 | async-start | bytes 5242880 | tf_op jit(solution)/shard_map/all_to_all | solution.py:164
  183.0 27.7 %all-to-all-done.1 = bf16[32,16,2560]{2,1,0:T(8,128)(2,1)} async-done(((bf16[32,16,2560]{2,1,0:T(8,128)(2,1)}), bf16[32,16,2560]{2,1,0:T(8,128)(2,1)}, u32[]{:S(2)}, u32[]{:S(2)}) %all-to-all-start.1) | async-done | bytes 2621472 | tf_op jit(solution)/shard_map/all_to_all | solution.py:164
  213.9 246.6 %while.10 = (s32[]{:T(128)}, bf16[4,64,2048]{2,1,0:T(8,128)(2,1)}, s32[4,64]{1,0:T(4,128)S(1)}, bf16[4,64,2048]{2,1,0:T(8,128)(2,1)S(1)}, s32[4,64,16]{2,1,0:T(8...) while((s32[]{:T(128)}, bf16[4,64,2048]{2,1,0:T(8,128)(2,1)}, ...), condition=%wide.region_13.14_spmd, body=%wide.region_10.13_spmd.sunk | while | flops 137014272 | bytes 90682720 | solution.py:189
  214.7 11.4 %gather_fusion.1 = bf16[1024,16,256]{2,1,0:T(8,128)(2,1)} fusion(bf16[320,16,256]{2,1,0:T(8,128)(2,1)} %get-tuple-element.213, s32[1024]{0:T(1024)S(1)} %broadcast_clamp_fusion.2), kind=kCustom, calls=%fused_computation.clone.1 | custom fusion | bytes 16781312 | tf_op jit(solution)/shard_map/while/body/eval_jaxpr/gather | solution.py:187
  226.1 12.5 %reshape.494 = bf16[64,256,2,128]{3,2,1,0:T(2,128)(2,1)} reshape(bf16[1024,16,256]{2,1,0:T(8,128)(2,1)} %gather_fusion.1) | data formatting | bytes 16777216 | tf_op jit(solution)/shard_map/while/body/eval_jaxpr/reshape | solution.py:83
  238.8 5.8 %fusion.91 = (f32[64,2,8]{2,1,0:T(2,128)S(1)}, f32[64,2,8,256]{3,2,1,0:T(8,128)S(1)}) fusion(bf16[64,2,8,128]{3,2,1,0:T(8,128)(2,1)S(1)} %bitcast.186, bf16[64,256,2,128]{3,2,1,0:T(2,128)(2,1)} %reshape.494, pred[64,256]{1,0:T(8,128)(4,1)S(1)} %iota_compare_fusion.12), kind=kOutput, calls=%fused_computation.129.clone.1 | convolution fusion | flops 67894272 | bytes 9719808 | tf_op jit(solution)/shard_map/while/body/eval_jaxpr/bhgd,bthd->bhgt/dot_general | solution.py:87
  246.0 11.4 %gather_fusion = bf16[1024,16,256]{2,1,0:T(8,128)(2,1)} fusion(bf16[320,16,256]{2,1,0:T(8,128)(2,1)} %get-tuple-element.215, s32[1024]{0:T(1024)S(1)} %broadcast_clamp_fusion.2), kind=kCustom, calls=%fused_computation.1.clone.1 | custom fusion | bytes 16781312 | tf_op jit(solution)/shard_map/while/body/eval_jaxpr/gather | solution.py:187
  257.4 12.5 %reshape.493 = bf16[64,256,2,128]{3,2,1,0:T(2,128)(2,1)} reshape(bf16[1024,16,256]{2,1,0:T(8,128)(2,1)} %gather_fusion) | data formatting | bytes 16777216 | tf_op jit(solution)/shard_map/while/body/eval_jaxpr/reshape | solution.py:84
  270.0 4.7 %fusion.96 = bf16[64,2,8,128]{3,2,1,0:T(8,128)(2,1)S(1)} fusion(bf16[64,256,2,128]{3,2,1,0:T(2,128)(2,1)} %reshape.493, f32[64,2,8,256]{3,2,1,0:T(8,128)S(1)} %get-tuple-element.184, f32[64,2,8]{2,1,0:T(2,128)S(1)} %copy.211, f32[64,2,8]{2,1,0:T(2,128)S(1)} %copy.209, f32[64,2,128]{2,1,0:T(2,128)S(1)} %reshape.496, f32[64,2,8]{2,1,0:T(2,128)S(1)} %copy.212), kind=kOutput, calls=%fused_computation.11.clone.1 | convolution fusion | flops 68288512 | bytes 9777152 | tf_op jit(solution)/shard_map/while/body/eval_jaxpr/bhgt,bthd->bhgd/dot_general | solution.py:105
  276.4 11.4 %gather_fusion.1 = bf16[1024,16,256]{2,1,0:T(8,128)(2,1)} fusion(bf16[320,16,256]{2,1,0:T(8,128)(2,1)} %get-tuple-element.213, s32[1024]{0:T(1024)S(1)} %broadcast_clamp_fusion.2), kind=kCustom, calls=%fused_computation.clone.1 | custom fusion | bytes 16781312 | tf_op jit(solution)/shard_map/while/body/eval_jaxpr/gather | solution.py:187
  287.8 12.5 %reshape.494 = bf16[64,256,2,128]{3,2,1,0:T(2,128)(2,1)} reshape(bf16[1024,16,256]{2,1,0:T(8,128)(2,1)} %gather_fusion.1) | data formatting | bytes 16777216 | tf_op jit(solution)/shard_map/while/body/eval_jaxpr/reshape | solution.py:83
  300.5 5.8 %fusion.91 = (f32[64,2,8]{2,1,0:T(2,128)S(1)}, f32[64,2,8,256]{3,2,1,0:T(8,128)S(1)}) fusion(bf16[64,2,8,128]{3,2,1,0:T(8,128)(2,1)S(1)} %bitcast.186, bf16[64,256,2,128]{3,2,1,0:T(2,128)(2,1)} %reshape.494, pred[64,256]{1,0:T(8,128)(4,1)S(1)} %iota_compare_fusion.12), kind=kOutput, calls=%fused_computation.129.clone.1 | convolution fusion | flops 67894272 | bytes 9719808 | tf_op jit(solution)/shard_map/while/body/eval_jaxpr/bhgd,bthd->bhgt/dot_general | solution.py:87
  307.6 11.4 %gather_fusion = bf16[1024,16,256]{2,1,0:T(8,128)(2,1)} fusion(bf16[320,16,256]{2,1,0:T(8,128)(2,1)} %get-tuple-element.215, s32[1024]{0:T(1024)S(1)} %broadcast_clamp_fusion.2), kind=kCustom, calls=%fused_computation.1.clone.1 | custom fusion | bytes 16781312 | tf_op jit(solution)/shard_map/while/body/eval_jaxpr/gather | solution.py:187
  319.0 12.5 %reshape.493 = bf16[64,256,2,128]{3,2,1,0:T(2,128)(2,1)} reshape(bf16[1024,16,256]{2,1,0:T(8,128)(2,1)} %gather_fusion) | data formatting | bytes 16777216 | tf_op jit(solution)/shard_map/while/body/eval_jaxpr/reshape | solution.py:84
  331.6 4.7 %fusion.96 = bf16[64,2,8,128]{3,2,1,0:T(8,128)(2,1)S(1)} fusion(bf16[64,256,2,128]{3,2,1,0:T(2,128)(2,1)} %reshape.493, f32[64,2,8,256]{3,2,1,0:T(8,128)S(1)} %get-tuple-element.184, f32[64,2,8]{2,1,0:T(2,128)S(1)} %copy.211, f32[64,2,8]{2,1,0:T(2,128)S(1)} %copy.209, f32[64,2,128]{2,1,0:T(2,128)S(1)} %reshape.496, f32[64,2,8]{2,1,0:T(2,128)S(1)} %copy.212), kind=kOutput, calls=%fused_computation.11.clone.1 | convolution fusion | flops 68288512 | bytes 9777152 | tf_op jit(solution)/shard_map/while/body/eval_jaxpr/bhgt,bthd->bhgd/dot_general | solution.py:105
  338.0 11.4 %gather_fusion.1 = bf16[1024,16,256]{2,1,0:T(8,128)(2,1)} fusion(bf16[320,16,256]{2,1,0:T(8,128)(2,1)} %get-tuple-element.213, s32[1024]{0:T(1024)S(1)} %broadcast_clamp_fusion.2), kind=kCustom, calls=%fused_computation.clone.1 | custom fusion | bytes 16781312 | tf_op jit(solution)/shard_map/while/body/eval_jaxpr/gather | solution.py:187
  349.4 12.5 %reshape.494 = bf16[64,256,2,128]{3,2,1,0:T(2,128)(2,1)} reshape(bf16[1024,16,256]{2,1,0:T(8,128)(2,1)} %gather_fusion.1) | data formatting | bytes 16777216 | tf_op jit(solution)/shard_map/while/body/eval_jaxpr/reshape | solution.py:83
  362.1 5.8 %fusion.91 = (f32[64,2,8]{2,1,0:T(2,128)S(1)}, f32[64,2,8,256]{3,2,1,0:T(8,128)S(1)}) fusion(bf16[64,2,8,128]{3,2,1,0:T(8,128)(2,1)S(1)} %bitcast.186, bf16[64,256,2,128]{3,2,1,0:T(2,128)(2,1)} %reshape.494, pred[64,256]{1,0:T(8,128)(4,1)S(1)} %iota_compare_fusion.12), kind=kOutput, calls=%fused_computation.129.clone.1 | convolution fusion | flops 67894272 | bytes 9719808 | tf_op jit(solution)/shard_map/while/body/eval_jaxpr/bhgd,bthd->bhgt/dot_general | solution.py:87
  369.2 11.4 %gather_fusion = bf16[1024,16,256]{2,1,0:T(8,128)(2,1)} fusion(bf16[320,16,256]{2,1,0:T(8,128)(2,1)} %get-tuple-element.215, s32[1024]{0:T(1024)S(1)} %broadcast_clamp_fusion.2), kind=kCustom, calls=%fused_computation.1.clone.1 | custom fusion | bytes 16781312 | tf_op jit(solution)/shard_map/while/body/eval_jaxpr/gather | solution.py:187
  380.7 12.5 %reshape.493 = bf16[64,256,2,128]{3,2,1,0:T(2,128)(2,1)} reshape(bf16[1024,16,256]{2,1,0:T(8,128)(2,1)} %gather_fusion) | data formatting | bytes 16777216 | tf_op jit(solution)/shard_map/while/body/eval_jaxpr/reshape | solution.py:84
  399.6 11.4 %gather_fusion.1 = bf16[1024,16,256]{2,1,0:T(8,128)(2,1)} fusion(bf16[320,16,256]{2,1,0:T(8,128)(2,1)} %get-tuple-element.213, s32[1024]{0:T(1024)S(1)} %broadcast_clamp_fusion.2), kind=kCustom, calls=%fused_computation.clone.1 | custom fusion | bytes 16781312 | tf_op jit(solution)/shard_map/while/body/eval_jaxpr/gather | solution.py:187
  411.1 12.5 %reshape.494 = bf16[64,256,2,128]{3,2,1,0:T(2,128)(2,1)} reshape(bf16[1024,16,256]{2,1,0:T(8,128)(2,1)} %gather_fusion.1) | data formatting | bytes 16777216 | tf_op jit(solution)/shard_map/while/body/eval_jaxpr/reshape | solution.py:83
  423.8 5.8 %fusion.91 = (f32[64,2,8]{2,1,0:T(2,128)S(1)}, f32[64,2,8,256]{3,2,1,0:T(8,128)S(1)}) fusion(bf16[64,2,8,128]{3,2,1,0:T(8,128)(2,1)S(1)} %bitcast.186, bf16[64,256,2,128]{3,2,1,0:T(2,128)(2,1)} %reshape.494, pred[64,256]{1,0:T(8,128)(4,1)S(1)} %iota_compare_fusion.12), kind=kOutput, calls=%fused_computation.129.clone.1 | convolution fusion | flops 67894272 | bytes 9719808 | tf_op jit(solution)/shard_map/while/body/eval_jaxpr/bhgd,bthd->bhgt/dot_general | solution.py:87
  430.9 11.4 %gather_fusion = bf16[1024,16,256]{2,1,0:T(8,128)(2,1)} fusion(bf16[320,16,256]{2,1,0:T(8,128)(2,1)} %get-tuple-element.215, s32[1024]{0:T(1024)S(1)} %broadcast_clamp_fusion.2), kind=kCustom, calls=%fused_computation.1.clone.1 | custom fusion | bytes 16781312 | tf_op jit(solution)/shard_map/while/body/eval_jaxpr/gather | solution.py:187
  442.3 12.5 %reshape.493 = bf16[64,256,2,128]{3,2,1,0:T(2,128)(2,1)} reshape(bf16[1024,16,256]{2,1,0:T(8,128)(2,1)} %gather_fusion) | data formatting | bytes 16777216 | tf_op jit(solution)/shard_map/while/body/eval_jaxpr/reshape | solution.py:84
  (175 shorter events, 62.1 us)
Async XLA Ops:
  0.0 2.0 copy-start
  0.0 13.7 %copy-start.8 = (s32[256]{0:T(256)S(1)}, s32[256]{0:T(256)}, u32[]{:S(2)}) copy-start(s32[256]{0:T(256)} %param.21) | copy-start | bytes 3076
  0.0 57.2 %copy-start.7 = (s32[512]{0:T(512)S(1)}, s32[512]{0:T(512)}, u32[]{:S(2)}) copy-start(s32[512]{0:T(512)} %param.22) | copy-start | bytes 6148
  4.0 112.0 %all-to-all-start = ((bf16[32,16,2048]{2,1,0:T(8,128)(2,1)}), bf16[32,16,2048]{2,1,0:T(8,128)(2,1)}, u32[]{:S(2)}, u32[]{:S(2)}) async-start(bf16[32,16,2048]{2,1,0:T(8,128)(2,1)} %bitcast.13), calls=%async_computation | async-start | bytes 4194304 | tf_op jit(solution)/shard_map/all_to_all | solution.py:154
  60.7 51.2 %copy-start.10 = (s32[32,2]{0,1:T(2,128)S(1)}, s32[32,2]{0,1:T(2,128)}, u32[]{:S(2)}) copy-start(s32[32,2]{0,1:T(2,128)} %param.20) | copy-start | bytes 772
  116.1 48.5 %all-to-all-start.2 = ((bf16[32,2,2,16,256]{4,3,1,2,0:T(8,128)(2,1)}), bf16[32,2,2,16,256]{4,3,1,2,0:T(8,128)(2,1)S(1)}, u32[]{:S(2)}, u32[]{:S(2)}) async-start(bf16[32,2,2,16,256]{4,3,1,2,0:T(8,128)(2,1)} %copy.139), calls=%async_computation.2 | async-start | bytes 2097152 | tf_op jit(solution)/shard_map/all_to_all | solution.py:155
  150.5 1.2 copy-start.11
  157.5 4.9 %copy-start.3 = (f32[32,16,256]{2,1,0:T(8,128)S(1)}, f32[32,16,256]{2,1,0:T(8,128)}, u32[]{:S(2)}) copy-start(f32[32,16,256]{2,1,0:T(8,128)} %fusion.29) | copy-start | bytes 1572868
  157.5 4.9 %copy-start.4 = (f32[32,16,256]{2,1,0:T(8,128)S(1)}, f32[32,16,256]{2,1,0:T(8,128)}, u32[]{:S(2)}) copy-start(f32[32,16,256]{2,1,0:T(8,128)} %fusion.32) | copy-start | bytes 1572868
  164.5 12.3 %copy-start.6 = (s32[256,16]{0,1:T(8,128)S(1)}, s32[256,16]{0,1:T(8,128)}, u32[]{:S(2)}) copy-start(s32[256,16]{0,1:T(8,128)} %param.18) | copy-start | bytes 49156
  164.5 13.0 %copy-start.9 = (s32[256]{0:T(256)S(1)}, s32[256]{0:T(256)}, u32[]{:S(2)}) copy-start(s32[256]{0:T(256)} %param.19) | copy-start | bytes 3076
  164.5 46.2 %all-to-all-start.1 = ((bf16[32,16,2560]{2,1,0:T(8,128)(2,1)}), bf16[32,16,2560]{2,1,0:T(8,128)(2,1)}, u32[]{:S(2)}, u32[]{:S(2)}) async-start(bf16[32,16,2560]{2,1,0:T(8,128)(2,1)} %fusion.23), calls=%async_computation.1 | async-start | bytes 5242880 | tf_op jit(solution)/shard_map/all_to_all | solution.py:164
  183.0 30.5 %copy-start.2 = (bf16[256,2048]{1,0:T(8,128)(2,1)S(1)}, bf16[256,2048]{1,0:T(8,128)(2,1)}, u32[]{:S(2)}) copy-start(bf16[256,2048]{1,0:T(8,128)(2,1)} %param.15) | copy-start | bytes 3145732
  210.7 3.1 copy-start.5
  460.4 1.2 copy-start.1
where the time goes:
time: 465 us; the launch traced here: 462 us
  local copies, waits for them, and re-layouts  242 us (52%)
  matrix products  66.4 us (14%)
  blocking collectives  60.7 us (13%)
  other arithmetic  37.5 us (8%)
  waiting for transfers between devices  27.7 us (6%)
  starting transfers between devices  26.1 us (6%)
    reshape x4, local copies, waits for them, and re-layouts, attend(): keys = key_pages.reshape(count, -1, heads_kv, HEAD_SIZE)  50.1 us
    reshape x4, local copies, waits for them, and re-layouts, attend(): values = value_pages.reshape(count, -1, heads_kv, HEAD_SIZE)  50.1 us
    gather x4, local copies, waits for them, and re-layouts, one_block(): value_store[t_blk]  45.7 us
    gather x4, local copies, waits for them, and re-layouts, one_block(): key_store[t_blk]  45.7 us
    all_gather x1, blocking collectives, shards(): all_ids = lax.all_gather(request_adapter, 'dp', axis=0, tiled=True)  43.5 us
    scatter x1, local copies, waits for them, and re-layouts, shards(): arriving_local = jnp.zeros((total_slots,), jnp.int32).at[where_to.reshape...  30.4 us
    all_to_all x1, waiting for transfers between devices, shards(): lax.all_to_all(update_delta.reshape(owners, capacity, query_part + 2 * kv...  27.7 us
    dot_general x4, matrix products, attend(): jnp.einsum('bhgd,bthd->bhgt', heads, keys, preferred_element_type=jnp.flo...  23.1 us
  transfers between devices with their start and end apart: 3, of which 1 were waited for; matrix products, arithmetic and copies ran while one was open for 20% of the time, Pallas kernels for 0%

commit v1 on v0

--- a/solution.py
+++ b/solution.py
@@ -1,8 +1,8 @@
-import math
-
 import jax
 import jax.numpy as jnp
 from jax import lax
+from jax.experimental import pallas as pl
+from jax.experimental.pallas import tpu as pltpu
 from jax.sharding import PartitionSpec as P
 
 HEAD_SIZE = 128
@@ -76,38 +76,63 @@
     ).astype(jnp.bfloat16)
 
 
-def attend(query, key_new, value_new, key_pages, value_pages, lengths):
-    count = query.shape[0]
-    heads_kv = key_new.shape[1] // HEAD_SIZE
-    groups = query.shape[1] // (heads_kv * HEAD_SIZE)
-    keys = key_pages.reshape(count, -1, heads_kv, HEAD_SIZE)
-    values = value_pages.reshape(count, -1, heads_kv, HEAD_SIZE)
-    heads = query.reshape(count, heads_kv, groups, HEAD_SIZE)
-    factor = HEAD_SIZE ** (-0.5)
-    scores = jnp.einsum("bhgd,bthd->bhgt", heads, keys, preferred_element_type=jnp.float32) * factor
-    own = (
-        jnp.einsum(
-            "bhgd,bhd->bhg",
-            heads,
-            key_new.reshape(count, heads_kv, HEAD_SIZE),
-            preferred_element_type=jnp.float32,
-        )
-        * factor
-    )
-    valid = jnp.arange(keys.shape[1], dtype=jnp.int32)[None, :] < lengths[:, None]
-    scores = jnp.where(valid[:, None, None, :], scores, -jnp.inf)
-    top = jnp.maximum(jnp.max(scores, axis=-1), own)
-    probs = jnp.exp(scores - top[..., None])
-    own_p = jnp.exp(own - top)
-    total = jnp.sum(probs, axis=-1) + own_p
-    weights = (probs / total[..., None]).astype(jnp.bfloat16)
-    own_w = (own_p / total).astype(jnp.bfloat16)
-    out = jnp.einsum("bhgt,bthd->bhgd", weights, values, preferred_element_type=jnp.float32)
-    out = out + own_w.astype(jnp.float32)[..., None] * value_new.reshape(
-        count, heads_kv, 1, HEAD_SIZE
-    ).astype(jnp.float32)
-    return out.reshape(count, -1).astype(jnp.bfloat16)
-
+def attend_kernel(table, lens, target_ref, back_ref, baseq_ref, basekv_ref, pool_ref, mig_ref, out_ref, ext, fresh, wide):
+    rows, heads = wide.shape[0], wide.shape[1]
+    pages, per = pool_ref.shape[0], table.shape[1]
+    D = 128; T = 16; group = 16
+    half = heads // 2
+    ext[:pages] = pool_ref[...]
+    ext[pages:] = mig_ref[...]
+    slots = back_ref.shape[0]
+    pick = (lax.broadcasted_iota(jnp.int32, (rows, slots), 1) == target_ref[...]).astype(jnp.bfloat16)
+    for h in range(heads):
+        part = jnp.dot(pick, back_ref[:, h*D:(h+1)*D], preferred_element_type=jnp.float32)
+        wide[:, h, :] = (baseq_ref[:, h*D:(h+1)*D].astype(jnp.float32) + part).astype(jnp.bfloat16).astype(jnp.float32)
+    part = jnp.dot(pick, back_ref[:, heads*D:], preferred_element_type=jnp.float32)
+    fresh[...] = (basekv_ref[...].astype(jnp.float32) + part).astype(jnp.bfloat16).astype(jnp.float32)
+    tok = lax.broadcasted_iota(jnp.int32, (heads, per*T), 1)
+    first = lax.broadcasted_iota(jnp.int32, (heads, D), 0) < half
+    scale = D ** -0.5
+    def gather(r, which):
+        return jnp.concatenate([ext[table[r, p], which] for p in range(per)], axis=0)
+    def two(r, at):
+        row = fresh[pl.ds(r, 1), at:at + 2*D]
+        return jnp.concatenate([jnp.broadcast_to(row[:, :D], (half, D)), jnp.broadcast_to(row[:, D:], (half, D))], axis=0)
+    def score(r):
+        q = wide[r]
+        zero = jnp.zeros_like(q)
+        both = jnp.concatenate([jnp.where(first, q, zero), jnp.where(first, zero, q)], axis=1).astype(jnp.bfloat16)
+        return lax.dot_general(both, gather(r, 0), (((1,), (1,)), ((), ())), preferred_element_type=jnp.float32)
+    def soft(r, s):
+        s = jnp.where(tok < lens[0, r], s * scale, -jnp.inf)
+        own = jnp.sum(wide[r] * two(r, 0), axis=1, keepdims=True) * scale
+        top = jnp.maximum(jnp.max(s, axis=1, keepdims=True), own)
+        p = jnp.exp(s - top)
+        po = jnp.exp(own - top)
+        inv = 1.0 / (jnp.sum(p, axis=1, keepdims=True) + po)
+        return (p * inv).astype(jnp.bfloat16), (po * inv).astype(jnp.bfloat16).astype(jnp.float32) * two(r, 2*D)
+    def weigh(r, p, ov):
+        o = jnp.dot(p, gather(r, 1), preferred_element_type=jnp.float32)
+        wide[r] = jnp.where(first, o[:, :D], o[:, D:]) + ov
+    def body(i, c):
+        ss = [score(i*group+j) for j in range(group)]
+        pp = [soft(i*group+j, ss[j]) for j in range(group)]
+        for j in range(group): weigh(i*group+j, *pp[j])
+        return c
+    lax.fori_loop(0, rows // group, body, 0)
+    for h in range(heads):
+        out_ref[:, h*D:(h+1)*D] = wide[:, h, :].astype(jnp.bfloat16)
+
+def attend(table, lens, target, back, baseq, basekv, pool, mig):
+    rows, width = baseq.shape
+    vm = pl.BlockSpec(memory_space=pltpu.VMEM)
+    sm = pl.BlockSpec(memory_space=pltpu.SMEM)
+    return pl.pallas_call(attend_kernel,
+        out_shape=jax.ShapeDtypeStruct((rows, width), jnp.bfloat16),
+        in_specs=[sm, sm] + [vm]*6, out_specs=vm,
+        scratch_shapes=[pltpu.VMEM((pool.shape[0]+mig.shape[0],)+pool.shape[1:], jnp.bfloat16), pltpu.VMEM(basekv.shape, jnp.float32), pltpu.VMEM((rows, width//128, 128), jnp.float32)],
+        compiler_params=pltpu.CompilerParams(vmem_limit_bytes=56*1024*1024),
+    )(table, lens, target, back, baseq, basekv, pool, mig)
 
 def shards(
     hidden,
@@ -136,25 +161,20 @@
     target = route_rows(slot_rows, owners, owner_grouping, capacity)
     placed = target[None, :] == jnp.arange(total_slots, dtype=jnp.int32)[:, None]
     placement = placed.astype(jnp.bfloat16)
-    send_rows = jnp.dot(placement, hidden, preferred_element_type=jnp.float32).astype(jnp.bfloat16)
-    send_rows = send_rows.reshape(owners, capacity, width_portion)
+    tags = jnp.broadcast_to(
+        (slot_rows % owner_grouping).astype(jnp.bfloat16)[:, None], (rows, HEAD_SIZE)
+    )
+    send_rows = jnp.dot(
+        placement, jnp.concatenate([hidden, tags], axis=1), preferred_element_type=jnp.float32
+    ).astype(jnp.bfloat16)
+    send_rows = send_rows.reshape(owners, capacity, width_portion + HEAD_SIZE)
     leaving_pages = key_value_pool[handover_pages]
-    all_ids = lax.all_gather(request_adapter, "dp", axis=0, tiled=True)
-    all_slots = lookup(all_ids, adapter_position).reshape(owners, rows)
-    all_targets = jax.vmap(lambda s: route_rows(s, owners, owner_grouping, capacity))(all_slots)
-    sources = jnp.arange(owners, dtype=jnp.int32)[:, None] * capacity
-    where_to = jnp.where(
-        all_slots // owner_grouping == me, all_targets % capacity + sources, total_slots
-    )
-    arriving_local = (
-        jnp.zeros((total_slots,), jnp.int32)
-        .at[where_to.reshape(-1)]
-        .set((all_slots % owner_grouping).reshape(-1), mode="drop")
-    )
     arrived = lax.all_to_all(send_rows, "dp", split_axis=0, concat_axis=0, tiled=True)
     migrated = lax.all_to_all(leaving_pages, "dp", split_axis=0, concat_axis=0, tiled=True)
+    arrived = arrived.reshape(total_slots, width_portion + HEAD_SIZE)
+    arriving_local = arrived[:, width_portion].astype(jnp.int32)
     update_delta = build_update_delta(
-        arrived.reshape(total_slots, width_portion),
+        arrived[:, :width_portion],
         arriving_local,
         adapter_down_weight,
         query_up_weight,
@@ -169,33 +189,16 @@
         tiled=True,
     )
     returned_flat = returned.reshape(total_slots, query_part + 2 * kv_part)
-    own_delta = lax.dot_general(
-        placement, returned_flat, (((0,), (0,)), ((), ())), preferred_element_type=jnp.float32
-    )
-    query = (base_query_rows.astype(jnp.float32) + own_delta[:, :query_part]).astype(jnp.bfloat16)
-    fresh = (
-        key_value_base.astype(jnp.float32) + own_delta[:, query_part:].reshape(rows, 2, kv_part)
-    ).astype(jnp.bfloat16)
-    arrived_pages = migrated.reshape(owners * MCAP, 2, PAGE_TOKENS, kv_part)
-    key_store = jnp.concatenate([key_value_pool[:, 0], arrived_pages[:, 0]], axis=0)
-    value_store = jnp.concatenate([key_value_pool[:, 1], arrived_pages[:, 1]], axis=0)
-    block = math.gcd(rows, 64)
-    count = rows // block
-
-    def one_block(call_arguments):
-        q_blk, f_blk, t_blk, l_blk = call_arguments
-        return attend(q_blk, f_blk[:, 0], f_blk[:, 1], key_store[t_blk], value_store[t_blk], l_blk)
-
-    out = lax.map(
-        one_block,
-        (
-            query.reshape(count, block, query_part),
-            fresh.reshape(count, block, 2, kv_part),
-            request_page_table.reshape(count, block, -1),
-            context_length.reshape(count, block),
-        ),
-    )
-    return out.reshape(rows, query_part)
+    return attend(
+        request_page_table,
+        context_length.reshape(1, rows),
+        target.reshape(rows, 1),
+        returned_flat,
+        base_query_rows,
+        key_value_base.reshape(rows, 2 * kv_part),
+        key_value_pool,
+        migrated.reshape(owners * MCAP, 2, PAGE_TOKENS, kv_part),
+    )
 
 
 def solution(mesh):

time: 465 us -> 171 us (0.37)
  local copies, waits for them, and re-layouts: 242 us -> 12.9 us
  matrix products: 66.4 us -> 22.4 us
  blocking collectives: 60.7 us -> 17.6 us
  other arithmetic: 37.5 us -> 7.86 us
  waiting for transfers between devices: 27.7 us -> 57.1 us
  Pallas kernels: 0 us -> 25.6 us
    reshape x10 -> x0, local copies, waits for them, and re-layouts: 100 us -> none  [the longest x4 50.1 us: attend(): keys = key_pages.reshape(count, -1, heads_kv, HEAD_SIZE)]
    gather x8 -> x0, local copies, waits for them, and re-layouts: 91.4 us -> none  [the longest x4 45.7 us: one_block(): value_store[t_blk]]
    dot_general x14 -> x1, matrix products: 47.6 us -> 3.39 us  [shards(): jnp.dot(placement, jnp.concatenate([hidden, tags], axis=1), preferred_ele...]
    all_gather x1 -> x0, blocking collectives: 43.5 us -> none  [shards(): all_ids = lax.all_gather(request_adapter, 'dp', axis=0, tiled=True)]
    scatter x1 -> x0, local copies, waits for them, and re-layouts: 30.4 us -> none  [shards(): arriving_local = jnp.zeros((total_slots,), jnp.int32).at[where_to.reshape...]
    all_to_all x1, waiting for transfers between devices: 0.01 us -> 25.7 us  [shards(): lax.all_to_all(send_rows, 'dp', split_axis=0, concat_axis=0, tiled=True)]
    pallas_call x0 -> x1, Pallas kernels: none -> 25.6 us  [attend(): pl.pallas_call(attend_kernel, out_shape=jax.ShapeDtypeStruct((rows, width...]
    another operation x4 -> x2, other arithmetic: 19.1 us -> 0.63 us
  transfers between devices with their start and end apart: 3 -> 3, of which waited for: 1 -> 2; matrix products, arithmetic and copies ran while one was open for 20% -> 21% of each run, Pallas kernels for 0% -> 0%
where the time goes in v1:
time: 171 us; the launch traced here: 170 us
  waiting for transfers between devices  57.1 us (33%)
  starting transfers between devices  26.6 us (16%)
  Pallas kernels  25.6 us (15%)
  matrix products  22.4 us (13%)
  blocking collectives  17.6 us (10%)
  local copies, waits for them, and re-layouts  12.9 us (8%)
  other arithmetic  7.86 us (5%)
    all_to_all x1, waiting for transfers between devices, shards(): lax.all_to_all(update_delta.reshape(owners, capacity, query_part + 2 * kv...  31.4 us
    all_to_all x1, waiting for transfers between devices, shards(): lax.all_to_all(send_rows, 'dp', split_axis=0, concat_axis=0, tiled=True)  25.7 us
    pallas_call x1, Pallas kernels, attend(): pl.pallas_call(attend_kernel, out_shape=jax.ShapeDtypeStruct((rows, width...  25.6 us
    psum x1, blocking collectives, shards(): lax.psum(partial_low, 'mp')  17.6 us
    all_to_all x1, starting transfers between devices, shards(): lax.all_to_all(update_delta.reshape(owners, capacity, query_part + 2 * kv...  12.3 us
    dot_general x1, matrix products, build_update_delta(): lax.dot_general(flattened_rows, flattened_down, (((1,), (1,)), ((), ())),...  10.6 us
    all_to_all x1, starting transfers between devices, shards(): lax.all_to_all(send_rows, 'dp', split_axis=0, concat_axis=0, tiled=True)  9.74 us
    dot_general x1, matrix products, build_update_delta(): jnp.dot(spread[:, :, 0, :].reshape(slots_in, owner_grouping * adapter_ran...  4.92 us
  transfers between devices with their start and end apart: 3, of which 2 were waited for; matrix products, arithmetic and copies ran while one was open for 21% of the time, Pallas kernels for 0%

profile of v1, /device:TPU:1, one launch (start us, length us, event | category | flops | bytes accessed | tf_op | source)
XLA Modules:
  0.0 170.1 jit_solution(11907675476804184233)
XLA Ops:
  0.0 0.9 select_reduce_fusion
  0.9 0.6 reduce-window.6
  1.5 0.2 slice_reduce_fusion
  2.0 3.4 %convolution_convert_fusion = bf16[512,2176]{1,0:T(8,128)(2,1)} fusion(bf16[256,128]{1,0:T(8,128)(2,1)S(1)} %broadcast_in_dim.18, bf16[256,2048]{1,0:T(8,128)(2,1)} %param.12, s32[256]{0:T(256)S(1)} %multiply_add_fusion), kind=kOutput, calls=%fused_computation.4 | convolution fusion | flops 573898752 | bytes 3343360 | tf_op jit(solution)/shard_map/dot_general | solution.py:167
  5.4 9.7 %all-to-all-start = ((bf16[32,16,2176]{2,1,0:T(8,128)(2,1)}), bf16[32,16,2176]{2,1,0:T(8,128)(2,1)S(1)}, u32[]{:S(2)}, u32[]{:S(2)}) async-start(bf16[32,16,2176]{2,1,0:T(8,128)(2,1)} %bitcast.5), calls=%async_computation | async-start | bytes 4456448 | tf_op jit(solution)/shard_map/all_to_all | solution.py:172
  15.4 3.8 %gather_fusion = bf16[64,2,16,256]{3,2,1,0:T(8,128)(2,1)} fusion(bf16[256,2,16,256]{3,2,1,0:T(8,128)(2,1)} %pool_ref.1, s32[1024]{0:T(1024)S(1)} %pad_clamp_fusion), kind=kCustom, calls=%fused_computation | custom fusion | bytes 2097408 | tf_op jit(solution)/shard_map/gather | solution.py:171
  19.1 25.7 %all-to-all-done = bf16[32,16,2176]{2,1,0:T(8,128)(2,1)S(1)} async-done(((bf16[32,16,2176]{2,1,0:T(8,128)(2,1)}), bf16[32,16,2176]{2,1,0:T(8,128)(2,1)S(1)}, u32[]{:S(2)}, u32[]{:S(2)}) %all-to-all-start) | async-done | bytes 2228256 | tf_op jit(solution)/shard_map/all_to_all | solution.py:172
  44.8 4.5 %all-to-all-start.2 = ((bf16[32,2,2,16,256]{4,3,2,1,0:T(8,128)(2,1)}), bf16[32,2,2,16,256]{4,3,2,1,0:T(8,128)(2,1)S(1)}, u32[]{:S(2)}, u32[]{:S(2)}) async-start(bf16[32,2,2,16,256]{4,3,2,1,0:T(8,128)(2,1)} %bitcast.23), calls=%async_computation.2 | async-start | bytes 2097152 | tf_op jit(solution)/shard_map/all_to_all | solution.py:173
  49.3 0.1 convert_reduce_fusion
  49.5 0.8 fusion.24
  50.3 0.7 copy.80
  51.0 10.6 %multiply_reduce_fusion = f32[512,192]{0,1:T(8,128)} fusion(f32[512,16]{0,1:T(8,128)} %copy.80, bf16[16,192,2048]{2,1,0:T(8,128)(2,1)} %bitcast.84, bf16[512,2176]{1,0:T(8,128)(2,1)S(1)} %bitcast.75), kind=kOutput, calls=%fused_computation.1 | convolution fusion | flops 6445498368 | bytes 15106048 | tf_op jit(solution)/shard_map/dot_general | solution.py:46
  61.5 17.6 %all-reduce.1 = bf16[512,192]{0,1:T(8,128)(2,1)S(1)} all-reduce(f32[512,192]{0,1:T(8,128)} %multiply_reduce_fusion), channel_id=1, replica_groups=mesh['dp'=32,'mp'=4] {'mp'}, use_global_device_ids=true, to_apply=%region_4.5 | all-reduce | flops 98304 | bytes 589824 | tf_op jit(solution)/shard_map/psum | solution.py:182
  79.1 0.2 copy.64
  79.4 2.4 %broadcast_multiply_fusion = bf16[512,16,3,64]{3,1,0,2:T(8,128)(2,1)S(1)} fusion(bf16[512,3,64]{2,0,1:T(8,128)(2,1)S(1)} %copy.64, bf16[512,16]{1,0:T(8,128)(2,1)S(1)} %copy-done.4), kind=kLoop, calls=%fused_computation.5 | loop fusion | flops 1572864 | bytes 3358720 | tf_op jit(solution)/shard_map/mul | solution.py:55
  81.8 1.1 fusion.31
  82.9 0.1 copy-done.8
  83.1 1.7 %fusion.5 = f32[32,16,256]{2,1,0:T(8,128)} fusion(bf16[32,16,16,64]{3,2,1,0:T(8,128)(2,1)S(1)} %bitcast.77, bf16[16,2,64,256]{3,2,1,0:T(8,128)(2,1)S(1)} %copy-done.8), kind=kOutput, calls=%fused_computation.11 | convolution fusion | flops 268435456 | bytes 3145728 | tf_op jit(solution)/shard_map/dot_general | solution.py:63
  84.8 1.7 %fusion.8 = f32[32,16,256]{2,1,0:T(8,128)} fusion(bf16[32,16,16,64]{3,2,1,0:T(8,128)(2,1)S(1)} %bitcast.76, bf16[16,2,64,256]{3,2,1,0:T(8,128)(2,1)S(1)} %copy-done.8), kind=kOutput, calls=%fused_computation.12 | convolution fusion | flops 268435456 | bytes 3145728 | tf_op jit(solution)/shard_map/dot_general | solution.py:68
  86.5 2.2 %dot_general.30 = bf16[32,16,1024]{2,1,0:T(8,128)(2,1)} reshape(bf16[512,16,1,64]{3,1,0,2:T(8,128)(2,1)S(1)} %get-tuple-element.5) | data formatting | bytes 2097152 | tf_op jit(solution)/shard_map/dot_general | solution.py:58
  88.8 4.9 %fusion.32 = f32[32,16,2048]{2,1,0:T(8,128)S(1)} fusion(bf16[32,16,1024]{2,1,0:T(8,128)(2,1)} %dot_general.30, bf16[1024,2048,1]{1,0,2:T(8,128)(2,1)} %bitcast.85), kind=kOutput, calls=%fused_computation.64 | convolution fusion | flops 2147483648 | bytes 9437184 | tf_op jit(solution)/shard_map/dot_general | solution.py:58
  93.7 2.1 %fusion = bf16[32,16,2560]{2,1,0:T(8,128)(2,1)} fusion(f32[32,16,256]{2,1,0:T(8,128)S(1)} %copy-done.3, f32[32,16,256]{2,1,0:T(8,128)S(1)} %copy-done.2, f32[32,16,2048]{2,1,0:T(8,128)S(1)} %fusion.32), kind=kLoop, calls=%fused_computation.3 | loop fusion | flops 5242880 | bytes 7864320 | tf_op jit(solution)/shard_map/convert_element_type | solution.py:76
  95.8 1.0 copy-done.1
  96.8 12.3 %all-to-all-start.1 = ((bf16[32,16,2560]{2,1,0:T(8,128)(2,1)}), bf16[32,16,2560]{2,1,0:T(8,128)(2,1)S(1)}, u32[]{:S(2)}, u32[]{:S(2)}) async-start(bf16[32,16,2560]{2,1,0:T(8,128)(2,1)} %fusion), calls=%async_computation.1 | async-start | bytes 5242880 | tf_op jit(solution)/shard_map/all_to_all | solution.py:184
  109.2 0.1 copy.63
  109.3 0.1 copy.57
  109.5 0.7 copy.83
  110.2 0.7 copy.70.table
  110.9 0.7 fusion.22.target_ref
  111.7 31.4 %all-to-all-done.1 = bf16[32,16,2560]{2,1,0:T(8,128)(2,1)S(1)} async-done(((bf16[32,16,2560]{2,1,0:T(8,128)(2,1)}), bf16[32,16,2560]{2,1,0:T(8,128)(2,1)S(1)}, u32[]{:S(2)}, u32[]{:S(2)}) %all-to-all-start.1) | async-done | bytes 2621472 | tf_op jit(solution)/shard_map/all_to_all | solution.py:184
  143.0 1.5 copy-done
  144.5 25.6 %shard_map.118 = bf16[256,2048]{1,0:T(8,128)(2,1)} custom-call(s32[256,16]{1,0:T(8,128)} %copy.70.table, s32[1,256]{1,0:T(1,128)} %bitcast.83, s32[256,1]{1,0:T(8,128)} %fusion.22.target_ref, bf16[512,2560]{1,0:T(8,128)(2,1)} %bitcast.72, bf16[256,2048]{1,0:T(8,128)(2,1)} %baseq_ref.1, bf16[256,512]{1,0:T(8,128)(2,1)} %bitcast.78, ...), custom_call_target="tpu_custom_call" | custom-call | tf_op jit(solution)/shard_map/pallas_call | solution.py:130
  (28 shorter events, 0.5 us)
Async XLA Ops:
  5.4 9.7 %copy-start.7 = (s32[32,2]{0,1:T(2,128)S(1)}, s32[32,2]{0,1:T(2,128)}, u32[]{:S(2)}) copy-start(s32[32,2]{0,1:T(2,128)} %param.18) | copy-start | bytes 772
  5.4 39.5 %all-to-all-start = ((bf16[32,16,2176]{2,1,0:T(8,128)(2,1)}), bf16[32,16,2176]{2,1,0:T(8,128)(2,1)S(1)}, u32[]{:S(2)}, u32[]{:S(2)}) async-start(bf16[32,16,2176]{2,1,0:T(8,128)(2,1)} %bitcast.5), calls=%async_computation | async-start | bytes 4456448 | tf_op jit(solution)/shard_map/all_to_all | solution.py:172
  44.8 51.0 %all-to-all-start.2 = ((bf16[32,2,2,16,256]{4,3,2,1,0:T(8,128)(2,1)}), bf16[32,2,2,16,256]{4,3,2,1,0:T(8,128)(2,1)S(1)}, u32[]{:S(2)}, u32[]{:S(2)}) async-start(bf16[32,2,2,16,256]{4,3,2,1,0:T(8,128)(2,1)} %bitcast.23), calls=%async_computation.2 | async-start | bytes 2097152 | tf_op jit(solution)/shard_map/all_to_all | solution.py:173
  51.0 28.4 %copy-start.4 = (bf16[512,16]{1,0:T(8,128)(2,1)S(1)}, bf16[512,16]{1,0:T(8,128)(2,1)}, u32[]{:S(2)}) copy-start(bf16[512,16]{1,0:T(8,128)(2,1)} %get-tuple-element.8) | copy-start | bytes 49156
  81.8 1.2 copy-start.8
  88.8 4.9 %copy-start.2 = (f32[32,16,256]{2,1,0:T(8,128)S(1)}, f32[32,16,256]{2,1,0:T(8,128)}, u32[]{:S(2)}) copy-start(f32[32,16,256]{2,1,0:T(8,128)} %fusion.5) | copy-start | bytes 1572868
  88.8 4.9 %copy-start.3 = (f32[32,16,256]{2,1,0:T(8,128)S(1)}, f32[32,16,256]{2,1,0:T(8,128)}, u32[]{:S(2)}) copy-start(f32[32,16,256]{2,1,0:T(8,128)} %fusion.8) | copy-start | bytes 1572868
  95.8 13.6 %copy-start.5 = (bf16[256,2,256]{2,1,0:T(2,128)(2,1)S(1)}, bf16[256,2,256]{2,1,0:T(2,128)(2,1)}, u32[]{:S(2)}) copy-start(bf16[256,2,256]{2,1,0:T(2,128)(2,1)} %param.14) | copy-start | bytes 786436
  95.8 14.4 %copy-start.6 = (s32[256,16]{0,1:T(8,128)S(1)}, s32[256,16]{0,1:T(8,128)}, u32[]{:S(2)}) copy-start(s32[256,16]{0,1:T(8,128)} %param.16) | copy-start | bytes 49156
  95.8 1.0 copy-start.1
  96.8 46.2 %all-to-all-start.1 = ((bf16[32,16,2560]{2,1,0:T(8,128)(2,1)}), bf16[32,16,2560]{2,1,0:T(8,128)(2,1)S(1)}, u32[]{:S(2)}, u32[]{:S(2)}) async-start(bf16[32,16,2560]{2,1,0:T(8,128)(2,1)} %fusion), calls=%async_computation.1 | async-start | bytes 5242880 | tf_op jit(solution)/shard_map/all_to_all | solution.py:184
  143.0 1.5 copy-start

commit v2 on v0

v2 whole, which is shorter than its diff:
```python
import jax
import jax.numpy as jnp
from jax import lax
from jax.experimental import pallas as pl
from jax.experimental.pallas import tpu as pltpu
from jax.sharding import PartitionSpec as P

HEAD_SIZE = 128
PAGE_TOKENS = 16
MCAP = 2
CAPACITY = 16
GROUP = 16
MESH = pl.DeviceIdType.MESH

adapter_scale = 0.5


def torus_offsets():
    near = [(1, 0), (0, 1), (3, 0), (0, 3)]
    diagonal = [(1, 1), (3, 3), (1, 3), (3, 1)]
    bent = [(2, 1), (1, 2), (2, 3), (3, 2)]
    straight = [(2, 0), (0, 2)]
    order = [(0, 0, 0), (0, 0, 1)]
    for chips in (near, diagonal, bent, straight, [(2, 2)]):
        for core in (0, 1):
            order += [(y, z, core) for y, z in chips]
    return order


OFFSETS = torus_offsets()
SENDS = [[(0, 0)], [(0, 1)], [(0, 2), (1, 0), (1, 1)], [(0, 3), (1, 2), (1, 3)]]


def fused(
    ids_hbm,
    place_hbm,
    table_hbm,
    lens_hbm,
    handover_hbm,
    hidden_hbm,
    base_query_hbm,
    base_kv_hbm,
    pool_hbm,
    down_hbm,
    query_up_hbm,
    kv_up_hbm,
    out_hbm,
    ids_row,
    place_row,
    table,
    lens,
    handover,
    out_ref,
    hidden,
    base_query,
    base_kv,
    base_new,
    down,
    query_up,
    kv_up,
    sent,
    arrived,
    leaving,
    landing,
    ext,
    low,
    part,
    gathered,
    delta,
    back,
    wide,
    fresh,
    load_sem,
    row_send,
    row_recv,
    page_send,
    page_recv,
    sum_send,
    sum_recv,
    back_send,
    back_recv,
):
    rows, width = hidden.shape
    slots = arrived.shape[0]
    owners = slots // CAPACITY
    adapters, _, rank, _ = down.shape
    pages = pool_hbm.shape[0]
    page_count = table.shape[0]
    D = HEAD_SIZE
    kv_heads = base_kv.shape[2] // D
    per_head = base_query.shape[1] // (kv_heads * D)
    chunk = (per_head + 2) * D
    blocks, packed = part.shape[0], part.shape[1]
    block = slots // blocks
    half_block = block // 2
    group_devices = block // CAPACITY

    loads = [
        pltpu.make_async_copy(hidden_hbm, hidden, load_sem.at[0]),
        pltpu.make_async_copy(pool_hbm, ext.at[pl.ds(0, pages)], load_sem.at[1]),
        pltpu.make_async_copy(down_hbm, down, load_sem.at[2]),
        pltpu.make_async_copy(query_up_hbm, query_up, load_sem.at[3]),
        pltpu.make_async_copy(kv_up_hbm, kv_up, load_sem.at[4]),
        pltpu.make_async_copy(base_query_hbm, base_query, load_sem.at[5]),
        pltpu.make_async_copy(base_kv_hbm, base_kv, load_sem.at[6]),
        pltpu.make_async_copy(ids_hbm, ids_row, load_sem.at[7]),
        pltpu.make_async_copy(place_hbm, place_row, load_sem.at[8]),
        pltpu.make_async_copy(handover_hbm, handover, load_sem.at[9]),
        pltpu.make_async_copy(table_hbm, table, load_sem.at[10]),
        pltpu.make_async_copy(lens_hbm, lens, load_sem.at[11]),
    ]
    for k in (7, 8, 0, 9, 1, 10, 11):
        loads[k].start()

    me = lax.axis_index("dp")
    mine = lax.axis_index("mp")
    y, z, core = me // 8, (me // 2) % 4, me % 2

    def ahead(o):
        return ((y + o[0]) % 4) * 8 + ((z + o[1]) % 4) * 2 + (core + o[2]) % 2

    def behind(o):
        return ((y + 4 - o[0]) % 4) * 8 + ((z + 4 - o[1]) % 4) * 2 + (core + o[2]) % 2

    def iota(shape, axis):
        return lax.broadcasted_iota(jnp.int32, shape, axis)

    barrier = pltpu.get_barrier_semaphore()
    for o in OFFSETS[1:]:
        pl.semaphore_signal(barrier, inc=1, device_id={"dp": ahead(o)}, device_id_type=MESH)
    for step in range(1, 4):
        pl.semaphore_signal(
            barrier, inc=1, device_id={"mp": (mine + step) % 4}, device_id_type=MESH
        )

    loads[7].wait()
    loads[8].wait()
    total = place_row.shape[1]
    first_index, second_index = iota((rows, rows), 0), iota((rows, rows), 1)
    diagonal = first_index == second_index
    ids_col = jnp.sum(jnp.where(diagonal, ids_row[...], 0), axis=1, keepdims=True)
    slot_col = jnp.sum(
        jnp.where(iota((rows, total), 1) == ids_col, place_row[...], 0), axis=1, keepdims=True
    )
    slot_row = jnp.sum(jnp.where(diagonal, slot_col, 0), axis=0, keepdims=True)
    shift = adapters.bit_length() - 1
    owner_row = lax.shift_right_logical(slot_row, shift)
    owner_col = lax.shift_right_logical(slot_col, shift)
    same = owner_col == owner_row
    rank_row = jnp.sum(
        jnp.where(same & (first_index < second_index), 1, 0), axis=0, keepdims=True
    )
    rank_col = jnp.sum(
        jnp.where(same & (second_index < first_index), 1, 0), axis=1, keepdims=True
    )
    target_row = owner_row * CAPACITY + rank_row
    target_col = owner_col * CAPACITY + rank_col
    tags = jnp.broadcast_to(
        (slot_col - owner_col * adapters).astype(jnp.float32), (rows, D)
    ).astype(jnp.bfloat16)

    loads[0].wait()
    for load in loads[2:7]:
        load.start()
    for b in range(4):
        piece = slots // 4
        placement = jnp.where(
            iota((piece, rows), 0) + b * piece == target_row, 1.0, 0.0
        ).astype(jnp.bfloat16)
        where = pl.ds(b * piece, piece)
        sent[where, width:] = jnp.dot(
            placement, tags, preferred_element_type=jnp.float32
        ).astype(jnp.bfloat16)

        def dispatch(c, carry, placement=placement, where=where):
            at = pl.ds(pl.multiple_of(c * 512, 512), 512)
            sent[where, at] = jnp.dot(
                placement, hidden[:, at], preferred_element_type=jnp.float32
            ).astype(jnp.bfloat16)
            return carry

        lax.fori_loop(0, width // 512, dispatch, 0)

    pl.semaphore_wait(barrier, len(OFFSETS) - 1 + 3)

    def rows_of(index):
        return pl.ds(pl.multiple_of(index * CAPACITY, CAPACITY), CAPACITY)

    row_copies = [None]
    for i, o in enumerate(OFFSETS):
        if i == 0:
            continue
        to = ahead(o)
        copy = pltpu.make_async_remote_copy(
            src_ref=sent.at[rows_of(to)],
            dst_ref=arrived.at[rows_of(i)],
            send_sem=row_send.at[i],
            recv_sem=row_recv.at[i],
            device_id={"dp": to},
            device_id_type=MESH,
        )
        copy.start()
        row_copies.append(copy)
    arrived[rows_of(0)] = sent[rows_of(me)]

    loads[1].wait()
    loads[9].wait()
    for d in range(owners):
        for m in range(MCAP):
            leaving[d * MCAP + m] = ext[handover[m, d]]

    page_copies = [None]
    for o in OFFSETS[1:]:
        to = ahead(o)
        i = len(page_copies)
        copy = pltpu.make_async_remote_copy(
            src_ref=leaving.at[pl.ds(to * MCAP, MCAP)],
            dst_ref=landing.at[pl.ds(me * MCAP, MCAP)],
            send_sem=page_send.at[i],
            recv_sem=page_recv.at[i],
            device_id={"dp": to},
            device_id_type=MESH,
        )
        copy.start()
        page_copies.append(copy)
    landing[pl.ds(me * MCAP, MCAP)] = leaving[pl.ds(me * MCAP, MCAP)]

    lane = iota((block, D), 1)
    left = lane < rank

    def wanted(b):
        tag = arrived[pl.ds(b * block, block), width:].astype(jnp.float32)
        return tag - jnp.where(left, 0.0, 1.0)

    def project(b):
        for i in range(b * group_devices, (b + 1) * group_devices):
            if i:
                row_copies[i].wait_recv()
        if b == 0:
            loads[2].wait()
        want = wanted(b)
        low[...] = jnp.zeros_like(low)

        def four(q, carry):
            x = arrived[pl.ds(b * block, block), :width]
            match = (q * 4).astype(jnp.float32)
            for j in range(3):
                weight = down[pl.ds(q * 4, 4), j].reshape(4 * rank, width)
                got = lax.dot_general(
                    x, weight, (((1,), (1,)), ((), ())), preferred_element_type=jnp.float32
                )
                low[j] += jnp.where(want == match, got[:, :D], 0.0) + jnp.where(
                    want == match + 2.0, got[:, D:], 0.0
                )
            return carry

        lax.fori_loop(0, adapters // 4, four, 0)
        both = [low[j] + pltpu.roll(low[j], rank, 1) for j in range(3)]
        part[b, :block] = jnp.where(left, both[0], both[1])
        part[b, block:] = jnp.where(
            left[:half_block], both[2][:half_block], both[2][half_block:]
        )
        copies = []
        for step in range(1, 4):
            copy = pltpu.make_async_remote_copy(
                src_ref=part.at[b],
                dst_ref=gathered.at[b, step - 1],
                send_sem=sum_send.at[b, step - 1],
                recv_sem=sum_recv.at[b, step - 1],
                device_id={"mp": (mine + step) % 4},
                device_id_type=MESH,
            )
            copy.start()
            copies.append(copy)
        return copies

    def back_copy(i, head):
        to = behind(OFFSETS[i])
        columns = pl.ds(head * chunk, chunk)
        return pltpu.make_async_remote_copy(
            src_ref=delta.at[rows_of(i), columns],
            dst_ref=back.at[rows_of(me), columns],
            send_sem=back_send.at[head, i],
            recv_sem=back_recv.at[head, i],
            device_id={"dp": to},
            device_id_type=MESH,
        )

    back_copies = {}

    def raise_up(b, copies):
        for copy in copies:
            copy.wait_recv()
        if b == 0:
            loads[3].wait()
            loads[4].wait()
        summed = (part[b] + gathered[b, 0]) + (gathered[b, 1] + gathered[b, 2])
        summed = summed.astype(jnp.bfloat16).astype(jnp.float32)
        first, second = summed[:block], summed[block:]
        first_turned = pltpu.roll(first, rank, 1)
        second_turned = pltpu.roll(second, rank, 1)
        half_left = left[:half_block]
        parts = [
            jnp.where(left, first, first_turned),
            jnp.where(left, first_turned, first),
            jnp.concatenate(
                [
                    jnp.where(half_left, second, second_turned),
                    jnp.where(half_left, second_turned, second),
                ],
                axis=0,
            ),
        ]
        want = wanted(b)
        spread = [
            jnp.concatenate(
                [
                    jnp.where(want == float(2 * p), one, 0.0).astype(jnp.bfloat16)
                    for p in range(adapters // 2)
                ],
                axis=1,
            )
            for one in parts
        ]
        here = pl.ds(b * block, block)
        depth = adapters * rank
        for head in range(kv_heads):
            start = head * per_head * D
            for c in range(0, per_head * D, 512):
                got = jnp.dot(
                    spread[0],
                    query_up[:, :, start + c : start + c + 512].reshape(depth, 512),
                    preferred_element_type=jnp.float32,
                )
                delta[here, head * chunk + c : head * chunk + c + 512] = (
                    adapter_scale * got
                ).astype(jnp.bfloat16)
        for j in range(2):
            got = jnp.dot(
                spread[1 + j],
                kv_up[:, j].reshape(depth, kv_heads * D),
                preferred_element_type=jnp.float32,
            )
            got = (adapter_scale * got).astype(jnp.bfloat16)
            for head in range(kv_heads):
                at = head * chunk + (per_head + j) * D
                delta[here, at : at + D] = got[:, head * D : (head + 1) * D]
        for head, which in SENDS[b]:
            for i in range(which * group_devices, (which + 1) * group_devices):
                if i == 0:
                    continue
                back_copies[head, i] = back_copy(i, head)
                back_copies[head, i].start()
        if b == 0:
            back[rows_of(me)] = delta[rows_of(0)]

    pending = None
    for b in range(blocks):
        started = project(b)
        if pending is not None:
            raise_up(b - 1, pending)
        pending = started
        if b == 0:
            sums = []
        sums.append(started)
    raise_up(blocks - 1, pending)

    for k in (5, 6, 10, 11):
        loads[k].wait()
    for k in range(2):
        base_new[:, k * kv_heads * D : (k + 1) * kv_heads * D] = base_kv[:, k, :].astype(
            jnp.float32
        )
    for i in range(1, len(OFFSETS)):
        page_copies[i].wait_recv()
    ext[pages:] = landing[...]

    pick = jnp.where(iota((rows, slots), 1) == target_col, 1.0, 0.0).astype(jnp.bfloat16)
    tokens = page_count * PAGE_TOKENS
    token = iota((per_head, tokens), 1)
    scale = D**-0.5

    def store(head):
        columns = pl.ds(head * per_head * D, per_head * D)
        return pltpu.make_async_copy(
            out_ref.at[:, columns], out_hbm.at[:, columns], load_sem.at[12 + head]
        )

    for head in range(kv_heads):
        for i in range(1, len(OFFSETS)):
            back_copies[head, i].wait_recv()
        for g in range(0, per_head + 2, 2):
            got = jnp.dot(
                pick,
                back[:, head * chunk + g * D : head * chunk + (g + 2) * D],
                preferred_element_type=jnp.float32,
            )
            for k in range(2):
                one = got[:, k * D : (k + 1) * D]
                if g < per_head:
                    at = (head * per_head + g + k) * D
                    base = base_query[:, at : at + D]
                else:
                    at = (k * kv_heads + head) * D
                    base = base_new[:, at : at + D]
                value = (base.astype(jnp.float32) + one).astype(jnp.bfloat16).astype(jnp.float32)
                if g < per_head:
                    wide[:, g + k, :] = value
                else:
                    fresh[:, k * D : (k + 1) * D] = value

        def gather(r, which, head=head):
            return jnp.concatenate(
                [
                    ext[table[p, r], which, :, head * D : (head + 1) * D]
                    for p in range(page_count)
                ],
                axis=0,
            )

        def score(r, gather=gather):
            return lax.dot_general(
                wide[r].astype(jnp.bfloat16),
                gather(r, 0),
                (((1,), (1,)), ((), ())),
                preferred_element_type=jnp.float32,
            )

        def soft(r, s):
            s = jnp.where(token < lens[0, r], s * scale, -jnp.inf)
            new = fresh[pl.ds(r, 1), :]
            own = jnp.sum(wide[r] * new[:, :D], axis=1, keepdims=True) * scale
            top = jnp.maximum(jnp.max(s, axis=1, keepdims=True), own)
            p = jnp.exp(s - top)
            po = jnp.exp(own - top)
            inv = 1.0 / (jnp.sum(p, axis=1, keepdims=True) + po)
            own_part = (po * inv).astype(jnp.bfloat16).astype(jnp.float32) * new[:, D:]
            return (p * inv).astype(jnp.bfloat16), own_part

        def weigh(r, p, own_part, gather=gather):
            wide[r] = jnp.dot(p, gather(r, 1), preferred_element_type=jnp.float32) + own_part

        def body(i, carry):
            at = i * GROUP
            scores = [score(at + j) for j in range(GROUP)]
            weights = [soft(at + j, scores[j]) for j in range(GROUP)]
            for j in range(GROUP):
                weigh(at + j, *weights[j])
            return carry

        lax.fori_loop(0, rows // GROUP, body, 0)
        for g in range(per_head):
            at = (head * per_head + g) * D
            out_ref[:, at : at + D] = wide[:, g, :].astype(jnp.bfloat16)
        store(head).start()

    for i in range(1, len(OFFSETS)):
        row_copies[i].wait_send()
        page_copies[i].wait_send()
        for head in range(kv_heads):
            back_copies[head, i].wait_send()
    for copies in sums:
        for copy in copies:
            copy.wait_send()
    for head in range(kv_heads):
        store(head).wait()


def shards(
    hidden,
    base_query_rows,
    key_value_base,
    key_value_pool,
    request_page_table,
    context_length,
    handover_pages,
    request_adapter,
    adapter_position,
    adapter_down_weight,
    query_up_weight,
    key_value_up,
):
    rows, width = hidden.shape
    owners = handover_pages.shape[0]
    slots = owners * CAPACITY
    query_part = base_query_rows.shape[1]
    kv_part = key_value_base.shape[2]
    kv_heads = kv_part // HEAD_SIZE
    per_head = query_part // kv_part
    total = adapter_position.shape[0]
    rank = adapter_down_weight.shape[2]
    blocks = 4
    block = slots // blocks
    packed = block * 3 // 2
    pages = key_value_pool.shape[0]
    bf16, f32 = jnp.bfloat16, jnp.float32
    hbm = pl.BlockSpec(memory_space=pl.ANY)
    dma = pltpu.SemaphoreType.DMA
    return pl.pallas_call(
        fused,
        out_shape=jax.ShapeDtypeStruct((rows, query_part), bf16),
        in_specs=[hbm] * 12,
        out_specs=hbm,
        scratch_shapes=[
            pltpu.VMEM((1, rows), jnp.int32),
            pltpu.VMEM((1, total), jnp.int32),
            pltpu.SMEM(request_page_table.shape[::-1], jnp.int32),
            pltpu.SMEM((1, rows), jnp.int32),
            pltpu.SMEM(handover_pages.shape[::-1], jnp.int32),
            pltpu.VMEM((rows, query_part), bf16),
            pltpu.VMEM((rows, width), bf16),
            pltpu.VMEM((rows, query_part), bf16),
            pltpu.VMEM(key_value_base.shape, bf16),
            pltpu.VMEM((rows, 2 * kv_part), f32),
            pltpu.VMEM(adapter_down_weight.shape, bf16),
            pltpu.VMEM(query_up_weight.shape, bf16),
            pltpu.VMEM(key_value_up.shape, bf16),
            pltpu.VMEM((slots, width + HEAD_SIZE), bf16),
            pltpu.VMEM((slots, width + HEAD_SIZE), bf16),
            pltpu.VMEM((owners * MCAP,) + key_value_pool.shape[1:], bf16),
            pltpu.VMEM((owners * MCAP,) + key_value_pool.shape[1:], bf16),
            pltpu.VMEM((pages + owners * MCAP,) + key_value_pool.shape[1:], bf16),
            pltpu.VMEM((3, block, HEAD_SIZE), f32),
            pltpu.VMEM((blocks, packed, HEAD_SIZE), f32),
            pltpu.VMEM((blocks, 3, packed, HEAD_SIZE), f32),
            pltpu.VMEM((slots, query_part + 2 * kv_part), bf16),
            pltpu.VMEM((slots, query_part + 2 * kv_part), bf16),
            pltpu.VMEM((rows, per_head, HEAD_SIZE), f32),
            pltpu.VMEM((rows, 2 * HEAD_SIZE), f32),
            dma((12 + kv_heads,)),
            dma((owners,)),
            dma((owners,)),
            dma((owners,)),
            dma((owners,)),
            dma((blocks, 3)),
            dma((blocks, 3)),
            dma((kv_heads, owners)),
            dma((kv_heads, owners)),
        ],
        compiler_params=pltpu.CompilerParams(
            collective_id=0, has_side_effects=True, vmem_limit_bytes=56 * 1024 * 1024
        ),
    )(
        request_adapter.reshape(1, rows),
        adapter_position.reshape(1, total),
        request_page_table.T,
        context_length.reshape(1, rows),
        handover_pages.T,
        hidden,
        base_query_rows,
        key_value_base,
        key_value_pool,
        adapter_down_weight,
        query_up_weight,
        key_value_up,
    )


def solution(mesh):
    return jax.shard_map(
        shards,
        mesh=mesh,
        in_specs=(
            P("dp", "mp"),
            P("dp", "mp"),
            P("dp", None, "mp"),
            P("dp", None, None, "mp"),
            P("dp", None),
            P("dp"),
            P("dp", None),
            P("dp"),
            P(),
            P("dp", None, None, "mp"),
            P("dp", None, "mp"),
            P("dp", None, None, "mp"),
        ),
        out_specs=P("dp", "mp"),
        check_vma=False,
    )
```

time: 465 us -> 109 us (0.23)
  local copies, waits for them, and re-layouts: 242 us -> 2.3 us
  Pallas kernels: 0 us -> 107 us
  matrix products: 66.4 us -> 0 us
  blocking collectives: 60.7 us -> 0 us
  other arithmetic: 37.5 us -> 0 us
  waiting for transfers between devices: 27.7 us -> 0 us
  starting transfers between devices: 26.1 us -> 0 us
    pallas_call x0 -> x1, Pallas kernels: none -> 107 us  [shards(): pl.pallas_call(fused, out_shape=jax.ShapeDtypeStruct((rows, query_part),...]
    reshape x10 -> x0, local copies, waits for them, and re-layouts: 100 us -> none  [the longest x4 50.1 us: attend(): keys = key_pages.reshape(count, -1, heads_kv, HEAD_SIZE)]
    gather x10 -> x0, local copies, waits for them, and re-layouts: 95.3 us -> none  [the longest x4 45.7 us: one_block(): value_store[t_blk]]
    dot_general x18 -> x0, matrix products: 66.4 us -> none  [the longest x4 23.1 us: attend(): jnp.einsum('bhgd,bthd->bhgt', heads, keys, preferred_element_type=jnp.flo...]
    all_gather x1 -> x0, blocking collectives: 43.5 us -> none  [shards(): all_ids = lax.all_gather(request_adapter, 'dp', axis=0, tiled=True)]
    scatter x1 -> x0, local copies, waits for them, and re-layouts: 30.4 us -> none  [shards(): arriving_local = jnp.zeros((total_slots,), jnp.int32).at[where_to.reshape...]
    all_to_all x3 -> x0, waiting for transfers between devices: 27.7 us -> none  [the longest x1 27.7 us: shards(): lax.all_to_all(update_delta.reshape(owners, capacity, query_part + 2 * kv...]
    all_to_all x3 -> x0, starting transfers between devices: 26.1 us -> none  [the longest x1 12.3 us: shards(): lax.all_to_all(update_delta.reshape(owners, capacity, query_part + 2 * kv...]
  transfers between devices with their start and end apart: 3 -> 0, of which waited for: 1 -> 0; matrix products, arithmetic and copies ran while one was open for 20% -> 0% of each run, Pallas kernels for 0% -> 0%
where the time goes in v2:
time: 109 us
  Pallas kernels  107 us (98%)
  local copies, waits for them, and re-layouts  2.3 us (2%)
    pallas_call x1, Pallas kernels, shards(): pl.pallas_call(fused, out_shape=jax.ShapeDtypeStruct((rows, query_part),...  107 us
    unnamed x1, local copies, waits for them, and re-layouts  2.3 us

profile of v2, /device:TPU:1, one launch (start us, length us, event | category | flops | bytes accessed | tf_op | source)
XLA Modules:
  0.0 108.9 jit_solution(9344601950267366777)
XLA Ops:
  0.0 106.5 %shard_map.118 = bf16[256,2048]{1,0:T(8,128)(2,1)} custom-call(s32[1,256]{1,0:T(1,128)} %bitcast.7, s32[1,512]{1,0:T(1,128)} %bitcast.6, s32[16,256]{1,0:T(8,128)} %bitcast.5, s32[1,256]{1,0:T(1,128)} %bitcast.8, s32[2,32]{1,0:T(2,128)} %bitcast.9, bf16[256,2048]{1,0:T(8,128)(2,1)} %hidden_hbm.1, bf16[256,2048]{1,0:T(8,128)(2,1)} %base_query_hbm.1, ...), custom_call_target="tpu_custom_call" | custom-call | tf_op jit(solution)/shard_map/pallas_call | solution.py:499
  106.5 2.3 %copy.14 = bf16[256,2048]{1,0:T(8,128)(2,1)} copy(bf16[256,2048]{1,0:T(8,128)(2,1)} %shard_map.118) | data formatting | bytes 2097152

commit v3 on v2

--- a/solution.py
+++ b/solution.py
@@ -377,7 +377,9 @@
 
     pick = jnp.where(iota((rows, slots), 1) == target_col, 1.0, 0.0).astype(jnp.bfloat16)
     tokens = page_count * PAGE_TOKENS
-    token = iota((per_head, tokens), 1)
+    heads = kv_heads * per_head
+    token = iota((heads, tokens), 1)
+    upper = iota((heads, D), 0) < per_head
     scale = D**-0.5
 
     def store(head):
@@ -405,53 +407,60 @@
                     base = base_new[:, at : at + D]
                 value = (base.astype(jnp.float32) + one).astype(jnp.bfloat16).astype(jnp.float32)
                 if g < per_head:
-                    wide[:, g + k, :] = value
+                    wide[:, head * per_head + g + k, :] = value
                 else:
-                    fresh[:, k * D : (k + 1) * D] = value
-
-        def gather(r, which, head=head):
-            return jnp.concatenate(
-                [
-                    ext[table[p, r], which, :, head * D : (head + 1) * D]
-                    for p in range(page_count)
-                ],
-                axis=0,
-            )
-
-        def score(r, gather=gather):
-            return lax.dot_general(
-                wide[r].astype(jnp.bfloat16),
-                gather(r, 0),
-                (((1,), (1,)), ((), ())),
-                preferred_element_type=jnp.float32,
-            )
-
-        def soft(r, s):
-            s = jnp.where(token < lens[0, r], s * scale, -jnp.inf)
-            new = fresh[pl.ds(r, 1), :]
-            own = jnp.sum(wide[r] * new[:, :D], axis=1, keepdims=True) * scale
-            top = jnp.maximum(jnp.max(s, axis=1, keepdims=True), own)
-            p = jnp.exp(s - top)
-            po = jnp.exp(own - top)
-            inv = 1.0 / (jnp.sum(p, axis=1, keepdims=True) + po)
-            own_part = (po * inv).astype(jnp.bfloat16).astype(jnp.float32) * new[:, D:]
-            return (p * inv).astype(jnp.bfloat16), own_part
-
-        def weigh(r, p, own_part, gather=gather):
-            wide[r] = jnp.dot(p, gather(r, 1), preferred_element_type=jnp.float32) + own_part
-
-        def body(i, carry):
-            at = i * GROUP
-            scores = [score(at + j) for j in range(GROUP)]
-            weights = [soft(at + j, scores[j]) for j in range(GROUP)]
-            for j in range(GROUP):
-                weigh(at + j, *weights[j])
-            return carry
-
-        lax.fori_loop(0, rows // GROUP, body, 0)
+                    fresh[:, at : at + D] = value
+
+    def gather(r, which):
+        return jnp.concatenate([ext[table[p, r], which] for p in range(page_count)], axis=0)
+
+    def per_row(r, at):
+        new = fresh[pl.ds(r, 1), at : at + 2 * D]
+        return jnp.concatenate(
+            [
+                jnp.broadcast_to(new[:, :D], (per_head, D)),
+                jnp.broadcast_to(new[:, D:], (per_head, D)),
+            ],
+            axis=0,
+        )
+
+    def score(r):
+        q = wide[r]
+        zero = jnp.zeros_like(q)
+        both = jnp.concatenate(
+            [jnp.where(upper, q, zero), jnp.where(upper, zero, q)], axis=1
+        ).astype(jnp.bfloat16)
+        return lax.dot_general(
+            both, gather(r, 0), (((1,), (1,)), ((), ())), preferred_element_type=jnp.float32
+        )
+
+    def soft(r, s):
+        s = jnp.where(token < lens[0, r], s * scale, -jnp.inf)
+        own = jnp.sum(wide[r] * per_row(r, 0), axis=1, keepdims=True) * scale
+        top = jnp.maximum(jnp.max(s, axis=1, keepdims=True), own)
+        p = jnp.exp(s - top)
+        po = jnp.exp(own - top)
+        inv = 1.0 / (jnp.sum(p, axis=1, keepdims=True) + po)
+        own_weight = (po * inv).astype(jnp.bfloat16).astype(jnp.float32)
+        return (p * inv).astype(jnp.bfloat16), own_weight * per_row(r, 2 * D)
+
+    def weigh(r, p, own_part):
+        o = jnp.dot(p, gather(r, 1), preferred_element_type=jnp.float32)
+        wide[r] = jnp.where(upper, o[:, :D], o[:, D:]) + own_part
+
+    def body(i, carry):
+        at = i * GROUP
+        scores = [score(at + j) for j in range(GROUP)]
+        weights = [soft(at + j, scores[j]) for j in range(GROUP)]
+        for j in range(GROUP):
+            weigh(at + j, *weights[j])
+        return carry
+
+    lax.fori_loop(0, rows // GROUP, body, 0)
+    for head in range(kv_heads):
         for g in range(per_head):
             at = (head * per_head + g) * D
-            out_ref[:, at : at + D] = wide[:, g, :].astype(jnp.bfloat16)
+            out_ref[:, at : at + D] = wide[:, head * per_head + g, :].astype(jnp.bfloat16)
         store(head).start()
 
     for i in range(1, len(OFFSETS)):
@@ -525,8 +534,8 @@
             pltpu.VMEM((blocks, 3, packed, HEAD_SIZE), f32),
             pltpu.VMEM((slots, query_part + 2 * kv_part), bf16),
             pltpu.VMEM((slots, query_part + 2 * kv_part), bf16),
-            pltpu.VMEM((rows, per_head, HEAD_SIZE), f32),
-            pltpu.VMEM((rows, 2 * HEAD_SIZE), f32),
+            pltpu.VMEM((rows, kv_heads * per_head, HEAD_SIZE), f32),
+            pltpu.VMEM((rows, 2 * kv_part), f32),
             dma((12 + kv_heads,)),
             dma((owners,)),
             dma((owners,)),

time: 109 us -> 103 us (0.945)
  Pallas kernels: 107 us -> 101 us
    pallas_call x1, Pallas kernels: 107 us -> 101 us  [shards(): pl.pallas_call(fused, out_shape=jax.ShapeDtypeStruct((rows, query_part),...]
where the time goes in v3:
time: 103 us
  Pallas kernels  101 us (98%)
  local copies, waits for them, and re-layouts  2.3 us (2%)
    pallas_call x1, Pallas kernels, shards(): pl.pallas_call(fused, out_shape=jax.ShapeDtypeStruct((rows, query_part),...  101 us
    unnamed x1, local copies, waits for them, and re-layouts  2.3 us

profile of v3, /device:TPU:1, one launch (start us, length us, event | category | flops | bytes accessed | tf_op | source)
XLA Modules:
  0.0 103.2 jit_solution(275553916200427314)
XLA Ops:
  0.0 100.9 %shard_map.118 = bf16[256,2048]{1,0:T(8,128)(2,1)} custom-call(s32[1,256]{1,0:T(1,128)} %bitcast.7, s32[1,512]{1,0:T(1,128)} %bitcast.6, s32[16,256]{1,0:T(8,128)} %bitcast.5, s32[1,256]{1,0:T(1,128)} %bitcast.8, s32[2,32]{1,0:T(2,128)} %bitcast.9, bf16[256,2048]{1,0:T(8,128)(2,1)} %hidden_hbm.1, bf16[256,2048]{1,0:T(8,128)(2,1)} %base_query_hbm.1, ...), custom_call_target="tpu_custom_call" | custom-call | tf_op jit(solution)/shard_map/pallas_call | solution.py:508
  100.9 2.3 %copy.14 = bf16[256,2048]{1,0:T(8,128)(2,1)} copy(bf16[256,2048]{1,0:T(8,128)(2,1)} %shard_map.118) | data formatting | bytes 2097152

commit v4 on v3

--- a/solution.py
+++ b/solution.py
@@ -9,7 +9,7 @@
 PAGE_TOKENS = 16
 MCAP = 2
 CAPACITY = 16
-GROUP = 16
+GROUP = 32
 MESH = pl.DeviceIdType.MESH
 
 adapter_scale = 0.5

time: 103 us -> 103 us (level)
  no operation moved by 1% of the time
where the time goes in v4:
time: 103 us
  Pallas kernels  100 us (97%)
  local copies, waits for them, and re-layouts  2.3 us (2%)
    pallas_call x1, Pallas kernels, shards(): pl.pallas_call(fused, out_shape=jax.ShapeDtypeStruct((rows, query_part),...  100 us
    unnamed x1, local copies, waits for them, and re-layouts  2.3 us

profile of v4, /device:TPU:1, one launch (start us, length us, event | category | flops | bytes accessed | tf_op | source)
XLA Modules:
  0.0 102.7 jit_solution(5222665829761022012)
XLA Ops:
  0.0 100.4 %shard_map.118 = bf16[256,2048]{1,0:T(8,128)(2,1)} custom-call(s32[1,256]{1,0:T(1,128)} %bitcast.7, s32[1,512]{1,0:T(1,128)} %bitcast.6, s32[16,256]{1,0:T(8,128)} %bitcast.5, s32[1,256]{1,0:T(1,128)} %bitcast.8, s32[2,32]{1,0:T(2,128)} %bitcast.9, bf16[256,2048]{1,0:T(8,128)(2,1)} %hidden_hbm.1, bf16[256,2048]{1,0:T(8,128)(2,1)} %base_query_hbm.1, ...), custom_call_target="tpu_custom_call" | custom-call | tf_op jit(solution)/shard_map/pallas_call | solution.py:508
  100.4 2.3 %copy.14 = bf16[256,2048]{1,0:T(8,128)(2,1)} copy(bf16[256,2048]{1,0:T(8,128)(2,1)} %shard_map.118) | data formatting | bytes 2097152
